TPU v7x, 32 devices: a whole 2x2x4 slice. The times are simulated.
32 devices in a mesh: seq: 8 (over z, x), tp: 4 (over y, core).
Axes of the slice: x: 2, y: 2, z: 4, core: 2. Of those that a mesh axis runs over, the one named last changes fastest.
Arguments:
- tokens: bfloat16 [16384, 1024], P('seq'), may hold values from -6 to 6
- cotangent: bfloat16 [16384, 1024], P('seq'), may hold values from -6 to 6
- start_flags: int32 [8], P('seq'), may hold values from 0 to 1, as said below
- gain_mixer: float32 [1024], replicated, may hold values from 0.5 to 1.5
- w_bgate: bfloat16 [1024, 1024], P(None, 'tp'), may hold values from -0.1875 to 0.1875
- w_cgate: bfloat16 [1024, 1024], P(None, 'tp'), may hold values from -0.1875 to 0.1875
- w_input: bfloat16 [1024, 1024], P(None, 'tp'), may hold values from -0.1875 to 0.1875
- conv_kernel: bfloat16 [3, 1024], P(None, 'tp'), may hold values from -3.5 to 3.5
- w_output: bfloat16 [1024, 1024], P('tp'), may hold values from -0.1875 to 0.1875
- gain_ffn: float32 [1024], replicated, may hold values from 0.5 to 1.5
- w_gate: bfloat16 [1024, 4608], P(None, 'tp'), may hold values from -0.1875 to 0.1875
- w_up: bfloat16 [1024, 4608], P(None, 'tp'), may hold values from -0.1875 to 0.1875
- w_down: bfloat16 [4608, 1024], P('tp'), may hold values from -0.09375 to 0.09375
- mean_gain_mixer: float32 [1024], replicated, may hold values from -16 to 16
- square_gain_mixer: float32 [1024], replicated, may hold values from 1 to 100
- mean_w_bgate: float32 [1024, 1024], P('seq', 'tp'), may hold values from -16 to 16
- square_w_bgate: float32 [1024, 1024], P('seq', 'tp'), may hold values from 1 to 100
- mean_w_cgate: float32 [1024, 1024], P('seq', 'tp'), may hold values from -16 to 16
- square_w_cgate: float32 [1024, 1024], P('seq', 'tp'), may hold values from 1 to 100
- mean_w_input: float32 [1024, 1024], P('seq', 'tp'), may hold values from -16 to 16
- square_w_input: float32 [1024, 1024], P('seq', 'tp'), may hold values from 1 to 100
- mean_conv_kernel: float32 [3, 1024], P(None, 'tp'), may hold values from -16 to 16
- square_conv_kernel: float32 [3, 1024], P(None, 'tp'), may hold values from 1 to 100
- mean_w_output: float32 [1024, 1024], P('tp', 'seq'), may hold values from -16 to 16
- square_w_output: float32 [1024, 1024], P('tp', 'seq'), may hold values from 1 to 100
- mean_gain_ffn: float32 [1024], replicated, may hold values from -16 to 16
- square_gain_ffn: float32 [1024], replicated, may hold values from 1 to 100
- mean_w_gate: float32 [1024, 4608], P('seq', 'tp'), may hold values from -16 to 16
- square_w_gate: float32 [1024, 4608], P('seq', 'tp'), may hold values from 1 to 100
- mean_w_up: float32 [1024, 4608], P('seq', 'tp'), may hold values from -16 to 16
- square_w_up: float32 [1024, 4608], P('seq', 'tp'), may hold values from 1 to 100
- mean_w_down: float32 [4608, 1024], P('tp', 'seq'), may hold values from -16 to 16
- square_w_down: float32 [4608, 1024], P('tp', 'seq'), may hold values from 1 to 100
Outputs:
- block_out: bfloat16 [16384, 1024], P('seq')
- grad_tokens: float32 [16384, 1024], P('seq')
- grad_gain_mixer: float32 [1024], replicated
- next_gain_mixer: float32 [1024], replicated
- mean_next_gain_mixer: float32 [1024], replicated
- square_next_gain_mixer: float32 [1024], replicated
- grad_w_bgate: float32 [1024, 1024], P('seq', 'tp')
- next_w_bgate: float32 [1024, 1024], P('seq', 'tp')
- mean_next_w_bgate: float32 [1024, 1024], P('seq', 'tp')
- square_next_w_bgate: float32 [1024, 1024], P('seq', 'tp')
- grad_w_cgate: float32 [1024, 1024], P('seq', 'tp')
- next_w_cgate: float32 [1024, 1024], P('seq', 'tp')
- mean_next_w_cgate: float32 [1024, 1024], P('seq', 'tp')
- square_next_w_cgate: float32 [1024, 1024], P('seq', 'tp')
- grad_w_input: float32 [1024, 1024], P('seq', 'tp')
- next_w_input: float32 [1024, 1024], P('seq', 'tp')
- mean_next_w_input: float32 [1024, 1024], P('seq', 'tp')
- square_next_w_input: float32 [1024, 1024], P('seq', 'tp')
- grad_conv_kernel: float32 [3, 1024], P(None, 'tp')
- next_conv_kernel: float32 [3, 1024], P(None, 'tp')
- mean_next_conv_kernel: float32 [3, 1024], P(None, 'tp')
- square_next_conv_kernel: float32 [3, 1024], P(None, 'tp')
- grad_w_output: float32 [1024, 1024], P('tp', 'seq')
- next_w_output: float32 [1024, 1024], P('tp', 'seq')
- mean_next_w_output: float32 [1024, 1024], P('tp', 'seq')
- square_next_w_output: float32 [1024, 1024], P('tp', 'seq')
- grad_gain_ffn: float32 [1024], replicated
- next_gain_ffn: float32 [1024], replicated
- mean_next_gain_ffn: float32 [1024], replicated
- square_next_gain_ffn: float32 [1024], replicated
- grad_w_gate: float32 [1024, 4608], P('seq', 'tp')
- next_w_gate: float32 [1024, 4608], P('seq', 'tp')
- mean_next_w_gate: float32 [1024, 4608], P('seq', 'tp')
- square_next_w_gate: float32 [1024, 4608], P('seq', 'tp')
- grad_w_up: float32 [1024, 4608], P('seq', 'tp')
- next_w_up: float32 [1024, 4608], P('seq', 'tp')
- mean_next_w_up: float32 [1024, 4608], P('seq', 'tp')
- square_next_w_up: float32 [1024, 4608], P('seq', 'tp')
- grad_w_down: float32 [4608, 1024], P('tp', 'seq')
- next_w_down: float32 [4608, 1024], P('tp', 'seq')
- mean_next_w_down: float32 [4608, 1024], P('tp', 'seq')
- square_next_w_down: float32 [4608, 1024], P('tp', 'seq')
Inputs may be any that keep to these rules, and one draw needn't show every extreme that they name: `start_flags`: the first shard's flag is 1; shards 1 and 5 have flag 0, so they continue the sequence of the shard before them.
All inputs are finite; a program needn't handle non-finite values.
Results may differ from a plain program's by a relative error of at most 0.0075.
The roundings to bfloat16 on the way count: a program that leaves them out, or rounds other values in their place, can miss the bound.
Values sent between devices are 32-bit elements; how exact they have to be, the bound alone decides.
No kernel may reach another device: no remote copies, remote signals or barrier semaphores. Data moves between devices by JAX's collectives and lax.ppermute only.
A program may use at most 192 MiB of HBM per device.

v0:
```python
import jax
import jax.numpy as jnp
from jax import lax
from jax.sharding import PartitionSpec as P

EPS = 1e-05


def shifted(block, axis, distance):
    devices = range(lax.axis_size(axis))
    route = [(i - distance, i) for i in devices if i - distance in devices]
    return lax.ppermute(block, axis, route)


def inner_rows(left, right):
    return lax.dot_general(
        left, right, (((0,), (0,)), ((), ())), preferred_element_type=jnp.float32
    )


def times_back(left, right):
    return lax.dot_general(
        left, right, (((1,), (1,)), ((), ())), preferred_element_type=jnp.float32
    )


def adamw(weight, grad, mean, square, decay, rate):
    mean_new = 0.9 * mean + 0.1 * grad
    square_new = 0.95 * square + 0.05 * grad * grad
    mean_hat = mean_new / (1.0 - 0.9**3)
    square_hat = square_new / (1.0 - 0.95**3)
    weight_new = weight - rate * (mean_hat / (jnp.sqrt(square_hat) + 1e-08) + decay * weight)
    return (weight_new, mean_new, square_new)


def norm_back(dnormed, normed, inverse):
    return inverse * (dnormed - normed * jnp.mean(dnormed * normed, axis=-1, keepdims=True))


def body(
    tokens,
    cotangent,
    start_flags,
    gain_mixer,
    w_bgate,
    w_cgate,
    w_input,
    conv_kernel,
    w_output,
    gain_ffn,
    w_gate,
    w_up,
    w_down,
    mean_gain_mixer,
    square_gain_mixer,
    mean_w_bgate,
    square_w_bgate,
    mean_w_cgate,
    square_w_cgate,
    mean_w_input,
    square_w_input,
    mean_conv_kernel,
    square_conv_kernel,
    mean_w_output,
    square_w_output,
    mean_gain_ffn,
    square_gain_ffn,
    mean_w_gate,
    square_w_gate,
    mean_w_up,
    square_w_up,
    mean_w_down,
    square_w_down,
):
    count = tokens.shape[0]
    xin = tokens.astype(jnp.float32)
    inverse_one = lax.rsqrt(jnp.mean(xin * xin, axis=-1, keepdims=True) + EPS)
    norm_one = xin * inverse_one
    hone = (norm_one * gain_mixer).astype(jnp.bfloat16)
    bgate = jnp.dot(hone, w_bgate, preferred_element_type=jnp.float32)
    cgate = jnp.dot(hone, w_cgate, preferred_element_type=jnp.float32)
    xval = jnp.dot(hone, w_input, preferred_element_type=jnp.float32)
    mixed_in = bgate * xval
    keeper = (1 - start_flags[0]).astype(jnp.float32)
    kernel = conv_kernel.astype(jnp.float32)
    previous = shifted(mixed_in[-2:], "seq", 1) * keeper
    extended = jnp.concatenate([previous, mixed_in], axis=0)
    conv = kernel[2] * mixed_in + kernel[1] * extended[1:-1] + kernel[0] * extended[:-2]
    gated = (cgate * conv).astype(jnp.bfloat16)
    mix = lax.psum(jnp.dot(gated, w_output, preferred_element_type=jnp.float32), "tp")
    resid = xin + mix
    inverse_two = lax.rsqrt(jnp.mean(resid * resid, axis=-1, keepdims=True) + EPS)
    norm_two = resid * inverse_two
    htwo = (norm_two * gain_ffn).astype(jnp.bfloat16)
    gate = jnp.dot(htwo, w_gate, preferred_element_type=jnp.float32)
    upval = jnp.dot(htwo, w_up, preferred_element_type=jnp.float32)
    sigma = jax.nn.sigmoid(gate)
    silu_gate = gate * sigma
    act = (silu_gate * upval).astype(jnp.bfloat16)
    ffn = lax.psum(jnp.dot(act, w_down, preferred_element_type=jnp.float32), "tp")
    block_out = (resid + ffn).astype(jnp.bfloat16)
    gout = cotangent.astype(jnp.float32)
    grad_down = inner_rows(act, cotangent)
    dact = times_back(cotangent, w_down)
    dgate = (dact * upval * (sigma * (1.0 + gate * (1.0 - sigma)))).astype(jnp.bfloat16)
    dupval = (dact * silu_gate).astype(jnp.bfloat16)
    grad_gate = inner_rows(htwo, dgate)
    grad_upw = inner_rows(htwo, dupval)
    dhtwo_part = times_back(dgate, w_gate) + times_back(dupval, w_up)
    dhtwo = lax.psum(dhtwo_part, "tp")
    dgain_ffn = jnp.sum(dhtwo * norm_two, axis=0)
    dresid = gout + norm_back(dhtwo * gain_ffn, norm_two, inverse_two)
    dmix = dresid.astype(jnp.bfloat16)
    grad_outw = inner_rows(gated, dmix)
    dgated = times_back(dmix, w_output)
    dcgate = (dgated * conv).astype(jnp.bfloat16)
    dconv = dgated * cgate
    dkernel = jnp.stack(
        [
            jnp.sum(dconv * extended[:-2], axis=0),
            jnp.sum(dconv * extended[1:-1], axis=0),
            jnp.sum(dconv * mixed_in, axis=0),
        ],
        axis=0,
    )
    dextended = (
        jnp.pad(kernel[2] * dconv, ((2, 0), (0, 0)))
        + jnp.pad(kernel[1] * dconv, ((1, 1), (0, 0)))
        + jnp.pad(kernel[0] * dconv, ((0, 2), (0, 0)))
    )
    returned = shifted(dextended[:2] * keeper, "seq", -1)
    dmixed = dextended[2:] + jnp.pad(returned, ((count - 2, 0), (0, 0)))
    dbgate = (dmixed * xval).astype(jnp.bfloat16)
    dxval = (dmixed * bgate).astype(jnp.bfloat16)
    grad_bw = inner_rows(hone, dbgate)
    grad_cw = inner_rows(hone, dcgate)
    grad_xw = inner_rows(hone, dxval)
    shared = (
        lax.psum_scatter(grad_bw, "seq", scatter_dimension=0, tiled=True),
        lax.psum_scatter(grad_cw, "seq", scatter_dimension=0, tiled=True),
        lax.psum_scatter(grad_xw, "seq", scatter_dimension=0, tiled=True),
        lax.psum_scatter(grad_outw, "seq", scatter_dimension=1, tiled=True),
        lax.psum_scatter(grad_gate, "seq", scatter_dimension=0, tiled=True),
        lax.psum_scatter(grad_upw, "seq", scatter_dimension=0, tiled=True),
        lax.psum_scatter(grad_down, "seq", scatter_dimension=1, tiled=True),
    )
    dhone_part = (
        times_back(dbgate, w_bgate) + times_back(dcgate, w_cgate) + times_back(dxval, w_input)
    )
    dhone = lax.psum(dhone_part, "tp")
    dgain_mixer = jnp.sum(dhone * norm_one, axis=0)
    grad_tokens = dresid + norm_back(dhone * gain_mixer, norm_one, inverse_one)
    small = lax.psum((dgain_mixer, dgain_ffn, dkernel), "seq")
    width = w_bgate.shape[0] // lax.axis_size("seq")
    offset = lax.axis_index("seq") * width

    def rows_of(weight):
        return lax.dynamic_slice_in_dim(weight, offset, width, 0).astype(jnp.float32)

    def columns_of(weight):
        return lax.dynamic_slice_in_dim(weight, offset, width, 1).astype(jnp.float32)

    params = [
        gain_mixer,
        rows_of(w_bgate),
        rows_of(w_cgate),
        rows_of(w_input),
        kernel,
        columns_of(w_output),
        gain_ffn,
        rows_of(w_gate),
        rows_of(w_up),
        columns_of(w_down),
    ]
    grads = [
        small[0],
        shared[0],
        shared[1],
        shared[2],
        small[2],
        shared[3],
        small[1],
        shared[4],
        shared[5],
        shared[6],
    ]
    moments = [
        (mean_gain_mixer, square_gain_mixer),
        (mean_w_bgate, square_w_bgate),
        (mean_w_cgate, square_w_cgate),
        (mean_w_input, square_w_input),
        (mean_conv_kernel, square_conv_kernel),
        (mean_w_output, square_w_output),
        (mean_gain_ffn, square_gain_ffn),
        (mean_w_gate, square_w_gate),
        (mean_w_up, square_w_up),
        (mean_w_down, square_w_down),
    ]
    decays = [0.0, 0.1, 0.1, 0.1, 0.1, 0.1, 0.0, 0.1, 0.1, 0.1]
    rates = [0.2, 0.01, 0.01, 0.01, 0.2, 0.01, 0.2, 0.01, 0.01, 0.01]
    outs = [block_out, grad_tokens]
    for index in range(10):
        weight_new, mean_new, square_new = adamw(
            params[index],
            grads[index],
            moments[index][0],
            moments[index][1],
            decays[index],
            rates[index],
        )
        outs = outs + [grads[index], weight_new, mean_new, square_new]
    return tuple(outs)


def solution(mesh):
    in_specs = (
        P("seq", None),
        P("seq", None),
        P("seq"),
        P(),
        P(None, "tp"),
        P(None, "tp"),
        P(None, "tp"),
        P(None, "tp"),
        P("tp", None),
        P(),
        P(None, "tp"),
        P(None, "tp"),
        P("tp", None),
        P(),
        P(),
        P("seq", "tp"),
        P("seq", "tp"),
        P("seq", "tp"),
        P("seq", "tp"),
        P("seq", "tp"),
        P("seq", "tp"),
        P(None, "tp"),
        P(None, "tp"),
        P("tp", "seq"),
        P("tp", "seq"),
        P(),
        P(),
        P("seq", "tp"),
        P("seq", "tp"),
        P("seq", "tp"),
        P("seq", "tp"),
        P("tp", "seq"),
        P("tp", "seq"),
    )
    out_specs = (
        P("seq", None),
        P("seq", None),
        P(),
        P(),
        P(),
        P(),
        P("seq", "tp"),
        P("seq", "tp"),
        P("seq", "tp"),
        P("seq", "tp"),
        P("seq", "tp"),
        P("seq", "tp"),
        P("seq", "tp"),
        P("seq", "tp"),
        P("seq", "tp"),
        P("seq", "tp"),
        P("seq", "tp"),
        P("seq", "tp"),
        P(None, "tp"),
        P(None, "tp"),
        P(None, "tp"),
        P(None, "tp"),
        P("tp", "seq"),
        P("tp", "seq"),
        P("tp", "seq"),
        P("tp", "seq"),
        P(),
        P(),
        P(),
        P(),
        P("seq", "tp"),
        P("seq", "tp"),
        P("seq", "tp"),
        P("seq", "tp"),
        P("seq", "tp"),
        P("seq", "tp"),
        P("seq", "tp"),
        P("seq", "tp"),
        P("tp", "seq"),
        P("tp", "seq"),
        P("tp", "seq"),
        P("tp", "seq"),
    )
    return jax.shard_map(body, mesh=mesh, in_specs=in_specs, out_specs=out_specs, check_vma=False)
```

profile of v0, /device:TPU:0, one launch (start us, length us, event | category | flops | bytes accessed | tf_op | source)
XLA Modules:
  0.0 1340.2 jit_solution(14432429471371438521)
XLA Ops:
  7.3 3.2 fusion.11
  13.7 2.6 fusion.52
  16.3 4.8 collective-permute-start
  22.5 3.5 multiply_convert_fusion.7
  26.0 4.7 fusion.54
  31.0 154.8 %all-reduce.10.cloned.1.call-done = f32[2048,1024]{1,0:T(8,128)} async-done(((f32[2048,1024]{1,0:T(8,128)}), f32[2048,1024]{1,0:T(8,128)}) %all-reduce.10.cloned.1.call-update) | async-done | bytes 8388624 | tf_op jit(solution)/shard_map/psum | solution.py:90
  185.8 5.7 multiply_reduce_fusion.2
  192.4 2.7 copy-done
  195.2 7.9 fusion.56
  203.1 7.9 fusion.55
  211.0 17.9 %multiply_convert_fusion = (bf16[2048,1152]{1,0:T(8,128)(2,1)}, bf16[2048,1152]{1,0:T(8,128)(2,1)}, bf16[2048,1152]{1,0:T(8,128)(2,1)}) fusion(f32[2048,1152]{1,0:T(8,128)} %fusion.55, f32[2048,1152]{1,0:T(8,128)} %fusion.56, bf16[2048,1024]{1,0:T(8,128)(2,1)} %param.34, bf16[1152,1024]{1,0:T(8,128)(2,1)} %param.45), kind=kOutput, calls=%fused_computation.7 | convolution fusion | flops 4867227648 | bytes 39583744 | tf_op jit(solution)/shard_map/dot_general | solution.py:22
  228.9 7.7 fusion.58
  236.6 8.5 convolution_add_fusion
  245.1 153.1 %all-reduce.12.cloned.1.call-done = f32[2048,1024]{1,0:T(8,128)} async-done(((f32[2048,1024]{1,0:T(8,128)}), f32[2048,1024]{1,0:T(8,128)}) %all-reduce.12.cloned.1.call-update) | async-done | bytes 8388624 | tf_op jit(solution)/shard_map/psum | solution.py:110
  398.3 7.1 multiply_reduce_fusion
  407.7 4.5 multiply_add_fusion
  412.2 3.4 copy-done.1
  415.6 2.3 fusion.13
  418.0 4.9 fusion.15
  422.9 2.2 multiply_reduce_fusion.5
  425.8 2.3 fusion.62
  428.8 2.0 collective-permute-start.1
  431.2 3.4 collective-permute-done.1
  435.1 1.6 copy-done.7
  436.7 2.2 fusion.63
  439.0 4.5 fusion.61
  443.6 10.3 fusion.64
  454.0 10.3 fusion.65
  464.4 9.7 fusion.66
  474.4 10.2 fusion.57
  487.2 4.7 add_add_fusion
  492.9 1.8 convert_subtract_fusion.3
  494.7 54.1 %reduce-scatter.10.cloned.1.call-done = f32[128,256]{1,0:T(8,128)} async-done(((f32[1024,256]{1,0:T(8,128)}), f32[128,256]{1,0:T(8,128)}) %reduce-scatter.10.cloned.1.call-update) | async-done | bytes 131088 | tf_op jit(solution)/shard_map/reduce_scatter | solution.py:140
  548.8 1.7 convert_subtract_fusion.5
  550.6 64.6 %reduce-scatter.12.cloned.1.call-done = f32[128,256]{1,0:T(8,128)} async-done(((f32[1024,256]{1,0:T(8,128)}), f32[128,256]{1,0:T(8,128)}) %reduce-scatter.12.cloned.1.call-update) | async-done | bytes 131088 | tf_op jit(solution)/shard_map/reduce_scatter | solution.py:141
  615.2 1.8 convert_subtract_fusion.4
  617.0 65.0 %reduce-scatter.8.cloned.1.call-done = f32[128,256]{1,0:T(8,128)} async-done(((f32[1024,256]{1,0:T(8,128)}), f32[128,256]{1,0:T(8,128)}) %reduce-scatter.8.cloned.1.call-update) | async-done | bytes 131088 | tf_op jit(solution)/shard_map/reduce_scatter | solution.py:139
  681.9 1.9 convert_subtract_fusion.6
  683.8 96.6 %reduce-scatter.16.cloned.1.call-done = f32[128,1152]{1,0:T(8,128)} async-done(((f32[1024,1152]{1,0:T(8,128)}), f32[128,1152]{1,0:T(8,128)}) %reduce-scatter.16.cloned.1.call-update) | async-done | bytes 589840 | tf_op jit(solution)/shard_map/reduce_scatter | solution.py:143
  780.4 2.6 convert_subtract_fusion.2
  783.1 96.6 %reduce-scatter.18.cloned.1.call-done = f32[128,1152]{1,0:T(8,128)} async-done(((f32[1024,1152]{1,0:T(8,128)}), f32[128,1152]{1,0:T(8,128)}) %reduce-scatter.18.cloned.1.call-update) | async-done | bytes 589840 | tf_op jit(solution)/shard_map/reduce_scatter | solution.py:144
  879.7 2.6 convert_subtract_fusion.1
  882.4 97.1 %reduce-scatter.20.cloned.1.call-done = f32[1152,128]{1,0:T(8,128)} async-done(((f32[1152,1024]{1,0:T(8,128)}), f32[1152,128]{1,0:T(8,128)}) %reduce-scatter.20.cloned.1.call-update) | async-done | bytes 589840 | tf_op jit(solution)/shard_map/reduce_scatter | solution.py:145
  979.5 2.8 convert_subtract_fusion
  982.3 288.3 %all-reduce.14.cloned.1.call-done = (f32[2048,1024]{1,0:T(8,128)}, f32[2048,1024]{1,0:T(8,128)}) async-done(((f32[2048,1024]{1,0:T(8,128)}, f32[2048,1024]{1,0:T(8,128)}), (f32[2048,1024]{1,0:T(8,128)}, f32[2048,1024]{1,0:T(8,128)})) %all-reduce.14.cloned.1.call-update) | async-done | bytes 16777232 | tf_op jit(solution)/shard_map/psum | solution.py:100
  1270.7 6.5 fusion.10
  1277.3 17.5 %fusion.9 = (f32[2048,1024]{1,0:T(8,128)}, bf16[2048,1024]{1,0:T(8,128)(2,1)}) fusion(f32[2048,1024]{1,0:T(8,128)} %copy-done.1, bf16[2048,1024]{1,0:T(8,128)(2,1)S(1)} %copy-done.3, f32[2048,1024]{1,0:T(8,128)} %get-tuple-element.53, f32[2048]{0:T(1024)S(1)} %broadcast_multiply_fusion.3, f32[1024]{0:T(1024)S(1)} %copy-done.36, f32[2048]{0:T(1024)S(1)} %copy-done.33, ...), kind=kLoop, calls=%fused_computation.16 | loop fusion | flops 18874368 | bytes 50352128 | tf_op jit(solution)/shard_map/add | solution.py:152
  1294.7 37.1 %all-reduce.4 = (f32[1024]{0:T(1024)S(1)}, f32[3,256]{1,0:T(4,128)S(1)}, f32[1024]{0:T(1024)S(1)}) all-reduce(f32[1024]{0:T(1024)S(1)} %get-tuple-element.44, f32[3,256]{1,0:T(4,128)S(1)} %pad_maximum_fusion.1, f32[1024]{0:T(1024)S(1)} %get-tuple-element.42), channel_id=1, replica_groups=mesh['seq'=8,'tp'=4] {'seq'}, use_global_device_ids=true, to_apply=%region_9.0 | all-reduce | flops 2816 | bytes 22528 | tf_op jit(solution)/shard_map/psum | solution.py:153
  (144 shorter events, 15.1 us)
Async XLA Ops:
  7.2 3.9 copy-start.35
  7.2 178.6 %all-reduce.10.cloned.1.call-start = ((), (), s32[]{:S(2)}) async-start(), calls=%async_computation.7 | async-start | bytes 16777216 | tf_op jit(solution)/shard_map/psum | solution.py:90
  7.3 3.9 copy-start.2
  12.3 10.2 copy-start.5
  13.7 7.5 copy-start.41
  13.7 8.8 copy-start.19
  16.3 6.1 collective-permute-start
  30.7 160.8 %copy-start.34 = (f32[1024]{0:T(1024)S(1)}, f32[1024]{0:T(1024)}, u32[]{:S(2)}) copy-start(f32[1024]{0:T(1024)} %param.42) | copy-start | bytes 12292
  30.7 367.5 %all-reduce.12.cloned.1.call-start = ((), (), s32[]{:S(2)}) async-start(), calls=%async_computation.8 | async-start | bytes 16777216 | tf_op jit(solution)/shard_map/psum | solution.py:110
  191.5 3.7 copy-start
  195.2 7.9 copy-start.13
  195.2 7.9 copy-start.37
  211.0 17.9 %copy-start.38 = (bf16[1024,1152]{1,0:T(8,128)(2,1)S(1)}, bf16[1024,1152]{1,0:T(8,128)(2,1)}, u32[]{:S(2)}) copy-start(bf16[1024,1152]{1,0:T(8,128)(2,1)} %param.43) | copy-start | bytes 7077892
  228.9 7.7 copy-start.40
  228.9 7.7 copy-start.52
  245.1 247.0 %reduce-scatter.14.cloned.1.call-start = ((), (), s32[]{:S(2)}) async-start(), calls=%async_computation.12 | async-start | bytes 1179648 | tf_op jit(solution)/shard_map/reduce_scatter | solution.py:142
  398.3 8.2 copy-start.4
  398.3 9.4 copy-start.12
  417.9 130.9 %reduce-scatter.10.cloned.1.call-start = ((), (), s32[]{:S(2)}) async-start(), calls=%async_computation.10 | async-start | bytes 1179648 | tf_op jit(solution)/shard_map/reduce_scatter | solution.py:140
  417.9 4.9 copy-start.17
  418.0 4.9 copy-start.18
  428.1 187.0 %reduce-scatter.12.cloned.1.call-start = ((), (), s32[]{:S(2)}) async-start(), calls=%async_computation.11 | async-start | bytes 1179648 | tf_op jit(solution)/shard_map/reduce_scatter | solution.py:141
  428.8 5.8 copy-start.9
  428.8 5.8 copy-start.10
  428.8 5.7 collective-permute-start.1
  439.0 243.0 %reduce-scatter.8.cloned.1.call-start = ((), (), s32[]{:S(2)}) async-start(), calls=%async_computation.9 | async-start | bytes 1179648 | tf_op jit(solution)/shard_map/reduce_scatter | solution.py:139
  443.6 336.9 %reduce-scatter.16.cloned.1.call-start = ((), (), s32[]{:S(2)}) async-start(), calls=%async_computation.13 | async-start | bytes 5308416 | tf_op jit(solution)/shard_map/reduce_scatter | solution.py:143
  453.9 425.8 %reduce-scatter.18.cloned.1.call-start = ((), (), s32[]{:S(2)}) async-start(), calls=%async_computation.14 | async-start | bytes 5308416 | tf_op jit(solution)/shard_map/reduce_scatter | solution.py:144
  464.4 515.1 %reduce-scatter.20.cloned.1.call-start = ((), (), s32[]{:S(2)}) async-start(), calls=%async_computation.15 | async-start | bytes 5308416 | tf_op jit(solution)/shard_map/reduce_scatter | solution.py:145
  474.2 796.5 %all-reduce.14.cloned.1.call-start = ((), (), s32[]{:S(2)}) async-start(), calls=%async_computation.16 | async-start | bytes 33554432 | tf_op jit(solution)/shard_map/psum | solution.py:100
  474.4 10.2 copy-start.20
  491.9 56.9 %copy-start.30 = (f32[128,256]{1,0:T(8,128)S(1)}, f32[128,256]{1,0:T(8,128)}, u32[]{:S(2)}) copy-start(f32[128,256]{1,0:T(8,128)} %param.50) | copy-start | bytes 393220
  491.9 56.9 %copy-start.31 = (f32[128,256]{1,0:T(8,128)S(1)}, f32[128,256]{1,0:T(8,128)}, u32[]{:S(2)}) copy-start(f32[128,256]{1,0:T(8,128)} %param.51) | copy-start | bytes 393220
  491.9 288.5 %copy-start.23 = (f32[128,1152]{1,0:T(8,128)S(1)}, f32[128,1152]{1,0:T(8,128)}, u32[]{:S(2)}) copy-start(f32[128,1152]{1,0:T(8,128)} %param.60) | copy-start | bytes 1769476
  492.0 288.5 %copy-start.24 = (f32[128,1152]{1,0:T(8,128)S(1)}, f32[128,1152]{1,0:T(8,128)}, u32[]{:S(2)}) copy-start(f32[128,1152]{1,0:T(8,128)} %param.61) | copy-start | bytes 1769476
  492.0 387.7 %copy-start.25 = (f32[128,1152]{1,0:T(8,128)S(1)}, f32[128,1152]{1,0:T(8,128)}, u32[]{:S(2)}) copy-start(f32[128,1152]{1,0:T(8,128)} %param.62) | copy-start | bytes 1769476
  492.0 387.7 %copy-start.26 = (f32[128,1152]{1,0:T(8,128)S(1)}, f32[128,1152]{1,0:T(8,128)}, u32[]{:S(2)}) copy-start(f32[128,1152]{1,0:T(8,128)} %param.63) | copy-start | bytes 1769476
  617.0 362.5 %copy-start.27 = (f32[1152,128]{1,0:T(8,128)S(1)}, f32[1152,128]{1,0:T(8,128)}, u32[]{:S(2)}) copy-start(f32[1152,128]{1,0:T(8,128)} %param.64) | copy-start | bytes 1769476
  783.1 487.6 %copy-start.33 = (f32[2048]{0:T(1024)S(1)}, f32[2048]{0:T(1024)}, u32[]{:S(2)}) copy-start(f32[2048]{0:T(1024)} %copy-done.32) | copy-start | bytes 24580
  783.1 487.6 %copy-start.36 = (f32[1024]{0:T(1024)S(1)}, f32[1024]{0:T(1024)}, u32[]{:S(2)}) copy-start(f32[1024]{0:T(1024)} %param.36) | copy-start | bytes 12292
  1270.7 6.5 copy-start.3
  1277.2 54.6 %copy-start.42 = (bf16[3,256]{1,0:T(4,128)(2,1)S(1)}, bf16[3,256]{1,0:T(4,128)(2,1)}, u32[]{:S(2)}) copy-start(bf16[3,256]{1,0:T(4,128)(2,1)} %param.40) | copy-start | bytes 4612
  1277.2 54.6 %copy-start.49 = (f32[3,256]{1,0:T(4,128)S(1)}, f32[3,256]{1,0:T(4,128)}, u32[]{:S(2)}) copy-start(f32[3,256]{1,0:T(4,128)} %param.54) | copy-start | bytes 9220
  1277.2 54.6 %copy-start.50 = (f32[3,256]{1,0:T(4,128)S(1)}, f32[3,256]{1,0:T(4,128)}, u32[]{:S(2)}) copy-start(f32[3,256]{1,0:T(4,128)} %param.55) | copy-start | bytes 9220
  1277.2 55.2 %copy-start.43 = (f32[1024]{0:T(1024)S(1)}, f32[1024]{0:T(1024)}, u32[]{:S(2)}) copy-start(f32[1024]{0:T(1024)} %param.58) | copy-start | bytes 12292
  1277.3 55.2 %copy-start.44 = (f32[1024]{0:T(1024)S(1)}, f32[1024]{0:T(1024)}, u32[]{:S(2)}) copy-start(f32[1024]{0:T(1024)} %param.59) | copy-start | bytes 12292
  1277.3 55.2 %copy-start.45 = (f32[1024]{0:T(1024)S(1)}, f32[1024]{0:T(1024)}, u32[]{:S(2)}) copy-start(f32[1024]{0:T(1024)} %param.47) | copy-start | bytes 12292
  1277.3 55.2 %copy-start.46 = (f32[1024]{0:T(1024)S(1)}, f32[1024]{0:T(1024)}, u32[]{:S(2)}) copy-start(f32[1024]{0:T(1024)} %param.46) | copy-start | bytes 12292
  (17 other events, 32.3 us)
Sparse Core Ops, SparseCore 0:
  30.8 154.9 all-reduce.9
  245.2 152.9 all-reduce.11
  418.0 64.0 reduce-scatter.13
  486.3 62.4 reduce-scatter.9
  552.6 62.4 reduce-scatter.11
  619.4 62.5 reduce-scatter.7
  686.2 94.2 reduce-scatter.15
  784.6 95.0 reduce-scatter.17
  884.0 95.4 reduce-scatter.19
  982.0 288.6 all-reduce.13
where the time goes:
time: 1350 us; the launch traced here: 1340 us
  waiting for transfers between devices  1070 us (79%)
  matrix products  126 us (9%)
  other arithmetic  66.7 us (5%)
  blocking collectives  37.1 us (3%)
  between operations  15.7 us (1%)
    psum x1, waiting for transfers between devices, body(): lax.psum(jnp.dot(act, w_down, preferred_element_type=jnp.float32), 'tp')  288 us
    psum x1, waiting for transfers between devices, body(): lax.psum(jnp.dot(gated, w_output, preferred_element_type=jnp.float32), 'tp')  155 us
    psum x1, waiting for transfers between devices, body(): dhtwo = lax.psum(dhtwo_part, 'tp')  153 us
    reduce_scatter x1, waiting for transfers between devices, body(): lax.psum_scatter(grad_down, 'seq', scatter_dimension=1, tiled=True)  97.1 us
    reduce_scatter x1, waiting for transfers between devices, body(): lax.psum_scatter(grad_upw, 'seq', scatter_dimension=0, tiled=True)  96.6 us
    reduce_scatter x1, waiting for transfers between devices, body(): lax.psum_scatter(grad_gate, 'seq', scatter_dimension=0, tiled=True)  96.6 us
    reduce_scatter x1, waiting for transfers between devices, body(): lax.psum_scatter(grad_bw, 'seq', scatter_dimension=0, tiled=True)  65 us
    reduce_scatter x1, waiting for transfers between devices, body(): lax.psum_scatter(grad_xw, 'seq', scatter_dimension=0, tiled=True)  64.6 us
  transfers between devices with their start and end apart: 12, of which 11 were waited for; matrix products, arithmetic and copies ran while one was open for 6% of the time, Pallas kernels for 0%

commit v1 on v0

--- a/solution.py
+++ b/solution.py
@@ -97,7 +97,9 @@
     sigma = jax.nn.sigmoid(gate)
     silu_gate = gate * sigma
     act = (silu_gate * upval).astype(jnp.bfloat16)
-    ffn = lax.psum(jnp.dot(act, w_down, preferred_element_type=jnp.float32), "tp")
+    ffn = jnp.sum(
+        lax.all_gather(jnp.dot(act, w_down, preferred_element_type=jnp.float32), "tp"), axis=0
+    )
     block_out = (resid + ffn).astype(jnp.bfloat16)
     gout = cotangent.astype(jnp.float32)
     grad_down = inner_rows(act, cotangent)

time: 1350 us -> 1390 us (1.030)
  waiting for transfers between devices: 1070 us -> 1100 us
  other arithmetic: 66.7 us -> 85.8 us
    all_gather x0 -> x1, waiting for transfers between devices: none -> 196 us  [body(): lax.all_gather(jnp.dot(act, w_down, preferred_element_type=jnp.float32),...]
    psum x1, waiting for transfers between devices: 288 us -> 153 us  [body(): dhone = lax.psum(dhone_part, 'tp')]
    reduce_scatter x1, waiting for transfers between devices: 96.6 us -> 28.8 us  [body(): lax.psum_scatter(grad_gate, 'seq', scatter_dimension=0, tiled=True)]
    reduce_scatter x1, waiting for transfers between devices: 0.02 us -> 64.6 us  [body(): lax.psum_scatter(grad_outw, 'seq', scatter_dimension=1, tiled=True)]
    psum x1, waiting for transfers between devices: 153 us -> 112 us  [body(): dhtwo = lax.psum(dhtwo_part, 'tp')]
    reduce_sum x0 -> x1, other arithmetic: none -> 17 us  [body(): jnp.sum(lax.all_gather(jnp.dot(act, w_down, preferred_element_type=jnp.fl...]
  transfers between devices with their start and end apart: 12 -> 13, of which waited for: 11 -> 13; matrix products, arithmetic and copies ran while one was open for 6% -> 9% of each run, Pallas kernels for 0% -> 0%
where the time goes in v1:
time: 1390 us; the launch traced here: 1380 us
  waiting for transfers between devices  1100 us (79%)
  matrix products  127 us (9%)
  other arithmetic  85.8 us (6%)
  blocking collectives  37.1 us (3%)
  between operations  15.4 us (1%)
    all_gather x1, waiting for transfers between devices, body(): lax.all_gather(jnp.dot(act, w_down, preferred_element_type=jnp.float32),...  196 us
    psum x1, waiting for transfers between devices, body(): lax.psum(jnp.dot(gated, w_output, preferred_element_type=jnp.float32), 'tp')  155 us
    psum x1, waiting for transfers between devices, body(): dhone = lax.psum(dhone_part, 'tp')  153 us
    psum x1, waiting for transfers between devices, body(): dhtwo = lax.psum(dhtwo_part, 'tp')  112 us
    reduce_scatter x1, waiting for transfers between devices, body(): lax.psum_scatter(grad_down, 'seq', scatter_dimension=1, tiled=True)  97 us
    reduce_scatter x1, waiting for transfers between devices, body(): lax.psum_scatter(grad_upw, 'seq', scatter_dimension=0, tiled=True)  96.4 us
    reduce_scatter x1, waiting for transfers between devices, body(): lax.psum_scatter(grad_cw, 'seq', scatter_dimension=0, tiled=True)  65.1 us
    reduce_scatter x1, waiting for transfers between devices, body(): lax.psum_scatter(grad_bw, 'seq', scatter_dimension=0, tiled=True)  65.1 us
  transfers between devices with their start and end apart: 13, of which 13 were waited for; matrix products, arithmetic and copies ran while one was open for 9% of the time, Pallas kernels for 0%

profile of v1, /device:TPU:0, one launch (start us, length us, event | category | flops | bytes accessed | tf_op | source)
XLA Modules:
  0.0 1384.1 jit_solution(11439404424124710429)
XLA Ops:
  7.3 3.2 fusion.11
  13.3 2.6 fusion.52
  15.9 4.8 collective-permute-start
  22.1 3.7 multiply_convert_fusion.7
  25.8 4.7 fusion.54
  30.7 154.8 %all-reduce.9.cloned.1.call-done = f32[2048,1024]{1,0:T(8,128)} async-done(((f32[2048,1024]{1,0:T(8,128)}), f32[2048,1024]{1,0:T(8,128)}) %all-reduce.9.cloned.1.call-update) | async-done | bytes 8388624 | tf_op jit(solution)/shard_map/psum | solution.py:90
  185.5 5.7 multiply_reduce_fusion.2
  192.2 2.7 copy-done.1
  194.9 7.9 fusion.56
  202.8 7.9 fusion.55
  210.7 17.9 %multiply_convert_fusion = (bf16[2048,1152]{1,0:T(8,128)(2,1)}, bf16[2048,1152]{1,0:T(8,128)(2,1)}, bf16[2048,1152]{1,0:T(8,128)(2,1)}) fusion(f32[2048,1152]{1,0:T(8,128)} %fusion.55, f32[2048,1152]{1,0:T(8,128)} %fusion.56, bf16[2048,1024]{1,0:T(8,128)(2,1)} %param.34, bf16[1152,1024]{1,0:T(8,128)(2,1)} %param.45), kind=kOutput, calls=%fused_computation.7 | convolution fusion | flops 4867227648 | bytes 39583744 | tf_op jit(solution)/shard_map/dot_general | solution.py:22
  228.6 7.7 fusion.58
  236.3 8.5 convolution_add_fusion
  244.9 10.1 fusion.57
  255.1 10.4 fusion.64
  265.6 10.3 fusion.65
  276.0 9.8 fusion.66
  285.9 112.1 %all-reduce.11.cloned.1.call-done = f32[2048,1024]{1,0:T(8,128)} async-done(((f32[2048,1024]{1,0:T(8,128)}), f32[2048,1024]{1,0:T(8,128)}) %all-reduce.11.cloned.1.call-update) | async-done | bytes 8388624 | tf_op jit(solution)/shard_map/psum | solution.py:112
  398.0 7.3 multiply_reduce_fusion
  405.3 195.9 %all-gather.3.cloned.1.call-done = f32[8192,1024]{1,0:T(8,128)} async-done(((f32[2048,1024]{1,0:T(8,128)}), f32[8192,1024]{1,0:T(8,128)}) %all-gather.3.cloned.1.call-update) | async-done | bytes 33554448 | tf_op jit(solution)/shard_map/all_gather | solution.py:101
  601.2 17.0 %reduce_sum.92 = f32[2048,1024]{1,0:T(8,128)} reduce(f32[4,2048,1024]{2,1,0:T(8,128)} %bitcast.48, f32[]{:T(128)} %constant.28.clone.1), dimensions={0}, to_apply=%region_3.0 | reduce | flops 6291456 | bytes 41943044 | tf_op jit(solution)/shard_map/reduce_sum | solution.py:100
  618.3 13.0 multiply_add_fusion
  631.2 3.4 copy-done
  634.6 2.3 fusion.13
  637.0 4.9 fusion.15
  642.3 2.2 multiply_reduce_fusion.5
  645.3 2.3 fusion.62
  650.2 3.8 collective-permute-done.1
  656.2 2.3 fusion.63
  658.8 4.5 fusion.61
  663.4 2.4 fusion.60
  667.1 4.7 add_add_fusion
  671.8 28.8 %reduce-scatter.16.cloned.1.call-done = f32[128,1152]{1,0:T(8,128)} async-done(((f32[1024,1152]{1,0:T(8,128)}), f32[128,1152]{1,0:T(8,128)}) %reduce-scatter.16.cloned.1.call-update) | async-done | bytes 589840 | tf_op jit(solution)/shard_map/reduce_scatter | solution.py:145
  700.6 2.6 convert_subtract_fusion.2
  703.3 96.4 %reduce-scatter.18.cloned.1.call-done = f32[128,1152]{1,0:T(8,128)} async-done(((f32[1024,1152]{1,0:T(8,128)}), f32[128,1152]{1,0:T(8,128)}) %reduce-scatter.18.cloned.1.call-update) | async-done | bytes 589840 | tf_op jit(solution)/shard_map/reduce_scatter | solution.py:146
  799.7 2.6 convert_subtract_fusion.1
  802.4 97.0 %reduce-scatter.20.cloned.1.call-done = f32[1152,128]{1,0:T(8,128)} async-done(((f32[1152,1024]{1,0:T(8,128)}), f32[1152,128]{1,0:T(8,128)}) %reduce-scatter.20.cloned.1.call-update) | async-done | bytes 589840 | tf_op jit(solution)/shard_map/reduce_scatter | solution.py:147
  899.4 3.0 convert_subtract_fusion
  902.4 64.6 %reduce-scatter.14.cloned.1.call-done = f32[256,128]{1,0:T(8,128)} async-done(((f32[256,1024]{1,0:T(8,128)}), f32[256,128]{1,0:T(8,128)}) %reduce-scatter.14.cloned.1.call-update) | async-done | bytes 131088 | tf_op jit(solution)/shard_map/reduce_scatter | solution.py:144
  967.0 1.7 convert_subtract_fusion.3
  968.8 65.1 %reduce-scatter.10.cloned.1.call-done = f32[128,256]{1,0:T(8,128)} async-done(((f32[1024,256]{1,0:T(8,128)}), f32[128,256]{1,0:T(8,128)}) %reduce-scatter.10.cloned.1.call-update) | async-done | bytes 131088 | tf_op jit(solution)/shard_map/reduce_scatter | solution.py:142
  1033.9 1.7 convert_subtract_fusion.5
  1035.6 64.8 %reduce-scatter.12.cloned.1.call-done = f32[128,256]{1,0:T(8,128)} async-done(((f32[1024,256]{1,0:T(8,128)}), f32[128,256]{1,0:T(8,128)}) %reduce-scatter.12.cloned.1.call-update) | async-done | bytes 131088 | tf_op jit(solution)/shard_map/reduce_scatter | solution.py:143
  1102.1 65.1 %reduce-scatter.8.cloned.1.call-done = f32[128,256]{1,0:T(8,128)} async-done(((f32[1024,256]{1,0:T(8,128)}), f32[128,256]{1,0:T(8,128)}) %reduce-scatter.8.cloned.1.call-update) | async-done | bytes 131088 | tf_op jit(solution)/shard_map/reduce_scatter | solution.py:141
  1169.0 152.6 %all-reduce.13.cloned.1.call-done = f32[2048,1024]{1,0:T(8,128)} async-done(((f32[2048,1024]{1,0:T(8,128)}), f32[2048,1024]{1,0:T(8,128)}) %all-reduce.13.cloned.1.call-update) | async-done | bytes 8388624 | tf_op jit(solution)/shard_map/psum | solution.py:152
  1321.6 5.8 fusion.10
  1327.4 37.1 %all-reduce.4 = (f32[1024]{0:T(1024)S(1)}, f32[3,256]{1,0:T(4,128)S(1)}, f32[1024]{0:T(1024)S(1)}) all-reduce(f32[1024]{0:T(1024)S(1)} %get-tuple-element.44, f32[3,256]{1,0:T(4,128)S(1)} %pad_maximum_fusion.1, f32[1024]{0:T(1024)S(1)} %get-tuple-element.42), channel_id=1, replica_groups=mesh['seq'=8,'tp'=4] {'seq'}, use_global_device_ids=true, to_apply=%region_9.0 | all-reduce | flops 2816 | bytes 22528 | tf_op jit(solution)/shard_map/psum | solution.py:155
  1365.8 11.6 fusion.9
  (166 shorter events, 17.3 us)
Async XLA Ops:
  7.2 178.3 %all-reduce.9.cloned.1.call-start = ((), (), s32[]{:S(2)}) async-start(), calls=%async_computation.7 | async-start | bytes 16777216 | tf_op jit(solution)/shard_map/psum | solution.py:90
  11.9 10.2 copy-start.3
  13.3 7.5 copy-start.42
  13.3 8.8 copy-start.18
  15.9 9.8 copy-start.6
  15.9 6.1 collective-permute-start
  30.5 160.8 %copy-start.35 = (f32[1024]{0:T(1024)S(1)}, f32[1024]{0:T(1024)}, u32[]{:S(2)}) copy-start(f32[1024]{0:T(1024)} %param.42) | copy-start | bytes 12292
  30.5 367.5 %all-reduce.11.cloned.1.call-start = ((), (), s32[]{:S(2)}) async-start(), calls=%async_computation.8 | async-start | bytes 16777216 | tf_op jit(solution)/shard_map/psum | solution.py:112
  194.9 7.9 copy-start.12
  194.9 7.9 copy-start.38
  210.7 17.9 %copy-start.39 = (bf16[1024,1152]{1,0:T(8,128)(2,1)S(1)}, bf16[1024,1152]{1,0:T(8,128)(2,1)}, u32[]{:S(2)}) copy-start(bf16[1024,1152]{1,0:T(8,128)(2,1)} %param.43) | copy-start | bytes 7077892
  228.6 7.7 copy-start.41
  228.6 7.7 copy-start.61
  244.8 356.4 %all-gather.3.cloned.1.call-start = ((), (), s32[]{:S(2)}) async-start(), calls=%async_computation.17 | async-start | bytes 41943040 | tf_op jit(solution)/shard_map/all_gather | solution.py:101
  255.0 445.6 %reduce-scatter.16.cloned.1.call-start = ((), (), s32[]{:S(2)}) async-start(), calls=%async_computation.14 | async-start | bytes 5308416 | tf_op jit(solution)/shard_map/reduce_scatter | solution.py:145
  265.5 534.2 %reduce-scatter.18.cloned.1.call-start = ((), (), s32[]{:S(2)}) async-start(), calls=%async_computation.15 | async-start | bytes 5308416 | tf_op jit(solution)/shard_map/reduce_scatter | solution.py:146
  275.9 623.5 %reduce-scatter.20.cloned.1.call-start = ((), (), s32[]{:S(2)}) async-start(), calls=%async_computation.16 | async-start | bytes 5308416 | tf_op jit(solution)/shard_map/reduce_scatter | solution.py:147
  285.8 681.2 %reduce-scatter.14.cloned.1.call-start = ((), (), s32[]{:S(2)}) async-start(), calls=%async_computation.13 | async-start | bytes 1179648 | tf_op jit(solution)/shard_map/reduce_scatter | solution.py:144
  637.0 396.9 %reduce-scatter.10.cloned.1.call-start = ((), (), s32[]{:S(2)}) async-start(), calls=%async_computation.11 | async-start | bytes 1179648 | tf_op jit(solution)/shard_map/reduce_scatter | solution.py:142
  647.6 452.8 %reduce-scatter.12.cloned.1.call-start = ((), (), s32[]{:S(2)}) async-start(), calls=%async_computation.12 | async-start | bytes 1179648 | tf_op jit(solution)/shard_map/reduce_scatter | solution.py:143
  648.2 5.8 copy-start.9
  648.3 5.8 collective-permute-start.1
  658.5 508.6 %reduce-scatter.8.cloned.1.call-start = ((), (), s32[]{:S(2)}) async-start(), calls=%async_computation.10 | async-start | bytes 1179648 | tf_op jit(solution)/shard_map/reduce_scatter | solution.py:141
  663.3 658.3 %all-reduce.13.cloned.1.call-start = ((), (), s32[]{:S(2)}) async-start(), calls=%async_computation.9 | async-start | bytes 16777216 | tf_op jit(solution)/shard_map/psum | solution.py:152
  671.8 28.8 %copy-start.21 = (f32[128,1152]{1,0:T(8,128)S(1)}, f32[128,1152]{1,0:T(8,128)}, u32[]{:S(2)}) copy-start(f32[128,1152]{1,0:T(8,128)} %param.60) | copy-start | bytes 1769476
  671.8 28.8 %copy-start.22 = (f32[128,1152]{1,0:T(8,128)S(1)}, f32[128,1152]{1,0:T(8,128)}, u32[]{:S(2)}) copy-start(f32[128,1152]{1,0:T(8,128)} %param.61) | copy-start | bytes 1769476
  671.8 128.0 %copy-start.23 = (f32[128,1152]{1,0:T(8,128)S(1)}, f32[128,1152]{1,0:T(8,128)}, u32[]{:S(2)}) copy-start(f32[128,1152]{1,0:T(8,128)} %param.62) | copy-start | bytes 1769476
  671.8 128.0 %copy-start.24 = (f32[128,1152]{1,0:T(8,128)S(1)}, f32[128,1152]{1,0:T(8,128)}, u32[]{:S(2)}) copy-start(f32[128,1152]{1,0:T(8,128)} %param.63) | copy-start | bytes 1769476
  703.3 263.8 %copy-start.25 = (f32[256,128]{1,0:T(8,128)S(1)}, f32[256,128]{1,0:T(8,128)}, u32[]{:S(2)}) copy-start(f32[256,128]{1,0:T(8,128)} %param.56) | copy-start | bytes 393220
  703.3 263.8 %copy-start.26 = (f32[256,128]{1,0:T(8,128)S(1)}, f32[256,128]{1,0:T(8,128)}, u32[]{:S(2)}) copy-start(f32[256,128]{1,0:T(8,128)} %param.57) | copy-start | bytes 393220
  703.3 330.6 %copy-start.27 = (f32[128,256]{1,0:T(8,128)S(1)}, f32[128,256]{1,0:T(8,128)}, u32[]{:S(2)}) copy-start(f32[128,256]{1,0:T(8,128)} %param.50) | copy-start | bytes 393220
  703.3 330.6 %copy-start.28 = (f32[128,256]{1,0:T(8,128)S(1)}, f32[128,256]{1,0:T(8,128)}, u32[]{:S(2)}) copy-start(f32[128,256]{1,0:T(8,128)} %param.51) | copy-start | bytes 393220
  703.3 397.1 %copy-start.29 = (f32[128,256]{1,0:T(8,128)S(1)}, f32[128,256]{1,0:T(8,128)}, u32[]{:S(2)}) copy-start(f32[128,256]{1,0:T(8,128)} %param.52) | copy-start | bytes 393220
  703.3 397.1 %copy-start.30 = (f32[128,256]{1,0:T(8,128)S(1)}, f32[128,256]{1,0:T(8,128)}, u32[]{:S(2)}) copy-start(f32[128,256]{1,0:T(8,128)} %param.53) | copy-start | bytes 393220
  703.3 463.9 %copy-start.31 = (f32[128,256]{1,0:T(8,128)S(1)}, f32[128,256]{1,0:T(8,128)}, u32[]{:S(2)}) copy-start(f32[128,256]{1,0:T(8,128)} %param.48) | copy-start | bytes 393220
  703.3 463.9 %copy-start.32 = (f32[128,256]{1,0:T(8,128)S(1)}, f32[128,256]{1,0:T(8,128)}, u32[]{:S(2)}) copy-start(f32[128,256]{1,0:T(8,128)} %param.49) | copy-start | bytes 393220
  802.4 519.2 %copy-start.34 = (f32[2048]{0:T(1024)S(1)}, f32[2048]{0:T(1024)}, u32[]{:S(2)}) copy-start(f32[2048]{0:T(1024)} %copy-done.33) | copy-start | bytes 24580
  802.4 519.2 %copy-start.37 = (f32[1024]{0:T(1024)S(1)}, f32[1024]{0:T(1024)}, u32[]{:S(2)}) copy-start(f32[1024]{0:T(1024)} %param.36) | copy-start | bytes 12292
  1168.9 195.6 %copy-start.43 = (bf16[3,256]{1,0:T(4,128)(2,1)S(1)}, bf16[3,256]{1,0:T(4,128)(2,1)}, u32[]{:S(2)}) copy-start(bf16[3,256]{1,0:T(4,128)(2,1)} %param.40) | copy-start | bytes 4612
  1168.9 195.6 %copy-start.58 = (f32[3,256]{1,0:T(4,128)S(1)}, f32[3,256]{1,0:T(4,128)}, u32[]{:S(2)}) copy-start(f32[3,256]{1,0:T(4,128)} %param.54) | copy-start | bytes 9220
  1168.9 195.6 %copy-start.59 = (f32[3,256]{1,0:T(4,128)S(1)}, f32[3,256]{1,0:T(4,128)}, u32[]{:S(2)}) copy-start(f32[3,256]{1,0:T(4,128)} %param.55) | copy-start | bytes 9220
  1168.9 196.2 %copy-start.52 = (f32[1024]{0:T(1024)S(1)}, f32[1024]{0:T(1024)}, u32[]{:S(2)}) copy-start(f32[1024]{0:T(1024)} %param.58) | copy-start | bytes 12292
  1168.9 196.2 %copy-start.53 = (f32[1024]{0:T(1024)S(1)}, f32[1024]{0:T(1024)}, u32[]{:S(2)}) copy-start(f32[1024]{0:T(1024)} %param.59) | copy-start | bytes 12292
  1169.0 196.2 %copy-start.54 = (f32[1024]{0:T(1024)S(1)}, f32[1024]{0:T(1024)}, u32[]{:S(2)}) copy-start(f32[1024]{0:T(1024)} %param.47) | copy-start | bytes 12292
  1169.0 196.2 %copy-start.55 = (f32[1024]{0:T(1024)S(1)}, f32[1024]{0:T(1024)}, u32[]{:S(2)}) copy-start(f32[1024]{0:T(1024)} %param.46) | copy-start | bytes 12292
  1364.5 12.9 copy-start.56
  1364.5 12.9 copy-start.57
  1364.5 12.9 copy-start.60
  (27 other events, 90.2 us)
Sparse Core Ops, SparseCore 0:
  30.6 154.8 all-reduce.8
  244.9 152.9 all-reduce.10
  399.5 201.6 all-gather.2
  605.3 95.2 reduce-scatter.15
  704.7 95.0 reduce-scatter.17
  803.8 95.5 reduce-scatter.19
  903.4 63.6 reduce-scatter.13
  971.4 62.4 reduce-scatter.9
  1037.9 62.4 reduce-scatter.11
  1104.6 62.5 reduce-scatter.7
  1169.6 151.8 all-reduce.12
